TPU v7x, 256 devices: a whole 4x4x8 slice. The times are simulated.
256 devices in a mesh: dp: 16 (over z, core), seq: 16 (over x, y).
Axes of the slice: x: 4, y: 4, z: 8, core: 2. Of those that a mesh axis runs over, the one named last changes fastest.
Arguments:
- query_rows: bfloat16 [16, 2048, 2048], P('dp', 'seq'), may hold values from -16 to 16
- key_rows: bfloat16 [16, 2048, 2048], P('dp', 'seq'), may hold values from -16 to 16
- value_rows: bfloat16 [16, 2048, 2048], P('dp', 'seq'), may hold values from -6 to 6
- out_cotangent: bfloat16 [16, 2048, 2048], P('dp', 'seq'), may hold values from -6 to 6
- segment_ids: int32 [16, 2048], P('dp'), may hold values from 0 to 7, never falling along the last dimension, each value on 1 to 1536 neighbouring positions
- gain_query: float32 [16, 128], P('seq'), may hold values from 0.5 to 6
- gain_key: float32 [16, 128], P('seq'), may hold values from 0.5 to 6
Outputs:
- attended: bfloat16 [16, 2048, 2048], P('dp', 'seq')
- grad_query: bfloat16 [16, 2048, 2048], P('dp', 'seq')
- grad_key: bfloat16 [16, 2048, 2048], P('dp', 'seq')
- grad_value: bfloat16 [16, 2048, 2048], P('dp', 'seq')
- grad_gain_query: float32 [16, 128], P('seq')
- grad_gain_key: float32 [16, 128], P('seq')
Inputs may be any that keep to these rules, and one draw needn't show every extreme that they name: `segment_ids`: image number of each token, never falling along the pack; each image with its prompt has 1 to 1536 tokens, one exactly 1536.
All inputs are finite; a program needn't handle non-finite values.
Results may differ from a plain program's by a relative error of at most 0.0065.
The roundings to bfloat16 on the way count: a program that leaves them out, or rounds other values in their place, can miss the bound.
Values may be sent and summed in bfloat16 or wider, within the bound.
A program may use at most 64 MiB of HBM per device.

v0:
```python
import functools
import math

import jax
import jax.numpy as jnp
from jax import lax
from jax.experimental import pallas as pl
from jax.experimental.pallas import tpu as pltpu
from jax.sharding import PartitionSpec as P

MESH = pl.DeviceIdType.MESH
EPSILON = 1e-06
NEGATIVE = -1e30
HD = 128
LEN = 2048
BIG = 1536
REST = LEN - BIG
ROWS = 256
SIDE = 4
SHARDS = SIDE * SIDE
TOK = LEN // SHARDS
SCALE = 1.0 / math.sqrt(HD)
EXP2_SCALE = SCALE * math.log2(math.e)
F32 = jnp.float32
BF16 = jnp.bfloat16


def dot_nt(a, b):
    return lax.dot_general(a, b, (((1,), (1,)), ((), ())), preferred_element_type=F32)


def dot_nn(a, b):
    return jnp.dot(a, b, preferred_element_type=F32)


def rows_at(start, size):
    return pl.ds(pl.multiple_of(start, size), size)


def kernel(
    dp_size,
    q_in, k_in, v_in, g_in, seg_s, seg_v, gain_q, gain_k,
    o_out, dq_out, dk_out, dv_out, ggq_out, ggk_out,
    rx, tx, shifted, qr, kr, vr, gr, q_t, g_t, marks, w_big, w_rest,
    go, gq, gk, gv, dk_t, dv_t, gains, gain_rx,
    in_send, in_recv, in_local, out_send, out_recv, out_local, gain_send, gain_recv,
):
    d = lax.axis_index("dp")
    me = lax.axis_index("seq")
    mx, my = me // SIDE, me % SIDE
    rounds = dp_size.bit_length() - 1

    def peer(j):
        return (mx + j // SIDE) % SIDE * SIDE + (my + j % SIDE) % SIDE

    def partner(r):
        bit = 1 << r
        return d + bit - 2 * bit * ((d // bit) % 2)

    barrier = pltpu.get_barrier_semaphore()

    def greet(j, carry):
        pl.semaphore_signal(barrier, inc=1, device_id=(d, peer(j)), device_id_type=MESH)
        return carry

    lax.fori_loop(1, SHARDS, greet, 0)
    for r in range(rounds):
        pl.semaphore_signal(barrier, inc=1, device_id=(partner(r), me), device_id_type=MESH)
    pl.semaphore_wait(barrier, SHARDS - 1 + rounds)

    sources = (q_in, k_in, v_in, g_in)
    targets = (o_out, dq_out, dk_out, dv_out)
    for a in range(4):

        def send(j, carry, a=a):
            to = peer(j)
            pltpu.make_async_remote_copy(
                src_ref=sources[a].at[0, :, rows_at(to * HD, HD)],
                dst_ref=rx.at[a, rows_at(me * TOK, TOK)],
                send_sem=in_send.at[a],
                recv_sem=in_recv.at[a],
                device_id=(d, to),
                device_id_type=MESH,
            ).start()
            return carry

        lax.fori_loop(1, SHARDS, send, 0)
        pltpu.make_async_copy(
            sources[a].at[0, :, rows_at(me * HD, HD)], rx.at[a, rows_at(me * TOK, TOK)], in_local.at[a]
        ).start()

    def arrived(a):
        part = rx.at[a, pl.ds(0, LEN - TOK)]
        pltpu.make_async_copy(part, part, in_recv.at[a]).wait()
        own = rx.at[a, pl.ds(0, TOK)]
        pltpu.make_async_copy(own, own, in_local.at[a]).wait()

    image = seg_s[0, LEN // 2]

    def halve(_, held):
        low, high = held
        mid = (low + high) // 2
        inside = seg_s[0, mid] >= image
        return (jnp.where(inside, low, mid + 1), jnp.where(inside, mid, high))

    first, _ = lax.fori_loop(0, 10, halve, (jnp.int32(0), jnp.int32(REST)))

    lanes = lax.broadcasted_iota(jnp.int32, (TOK, HD), 1).astype(F32)
    for t in range(2 * REST // TOK):
        token = (BIG + t * TOK) % LEN
        numbers = seg_v[0:1, token : token + TOK].astype(F32)
        column = jnp.broadcast_to(numbers, (HD, TOK)).T
        shifted[t * TOK : (t + 1) * TOK] = jnp.where(column == lanes, 1.0, 0.0)
    marks[...] = shifted[pl.ds(first, REST), :].astype(BF16)

    def wrap():
        shifted[LEN : LEN + REST] = shifted[0:REST]

    def norm_parts(a, at):
        x = rx[a, at, :].astype(F32)
        inverse = lax.rsqrt(jnp.mean(x * x, axis=1, keepdims=True) + EPSILON)
        return x * inverse, inverse

    def fill(a, gain):

        def body(b, carry):
            at = rows_at(b * ROWS, ROWS)
            if gain is None:
                shifted[at, :] = rx[a, at, :].astype(F32)
            else:
                shifted[at, :] = norm_parts(a, at)[0] * gain[...]
            return carry

        lax.fori_loop(0, LEN // ROWS, body, 0)
        wrap()

    def roll_into(rolled, turned):

        def body(b, carry):
            value = shifted[pl.ds(first + b * ROWS, ROWS), :]
            rolled[rows_at(b * ROWS, ROWS), :] = value.astype(BF16)
            if turned is not None:
                turned[:, rows_at(b * ROWS, ROWS)] = value.T.astype(BF16)
            return carry

        lax.fori_loop(0, LEN // ROWS, body, 0)

    arrived(0)
    fill(0, gain_q)
    roll_into(qr, q_t)
    arrived(1)
    fill(1, gain_k)
    roll_into(kr, None)

    def weights_of(scores):
        top = jnp.max(scores, axis=1, keepdims=True)
        powers = jnp.exp2((scores - top) * EXP2_SCALE)
        return powers * (1.0 / jnp.sum(powers, axis=1, keepdims=True))

    def big_weights(b, carry):
        at = rows_at(b * ROWS, ROWS)
        w_big[at, :] = weights_of(dot_nt(qr[at, :], kr[0:BIG, :]))
        return carry

    lax.fori_loop(0, BIG // ROWS, big_weights, 0)

    def rest_weights(b, carry):
        at = rows_at(b * ROWS, ROWS)
        scores = dot_nt(qr[rows_at(BIG + b * ROWS, ROWS), :], kr[BIG:LEN, :])
        allowed = dot_nt(marks[at, :], marks[...]) > 0.5
        w_rest[at, :] = weights_of(jnp.where(allowed, scores, NEGATIVE))
        return carry

    lax.fori_loop(0, REST // ROWS, rest_weights, 0)

    arrived(2)
    fill(2, None)
    roll_into(vr, None)

    def big_values(b, carry):
        at = rows_at(b * ROWS, ROWS)
        go[rows_at(REST + b * ROWS, ROWS), :] = dot_nn(w_big[at, :].astype(BF16), vr[0:BIG, :])
        return carry

    lax.fori_loop(0, BIG // ROWS, big_values, 0)

    def rest_values(b, carry):
        at = rows_at(b * ROWS, ROWS)
        value = dot_nn(w_rest[at, :].astype(BF16), vr[BIG:LEN, :])
        go[rows_at(LEN + b * ROWS, ROWS), :] = value
        go[at, :] = value
        return carry

    lax.fori_loop(0, REST // ROWS, rest_values, 0)

    def send_back(a, t):
        @pl.when(t != me)
        def _():
            pltpu.make_async_remote_copy(
                src_ref=tx.at[a, rows_at(t * TOK, TOK)],
                dst_ref=targets[a].at[0, :, rows_at(me * HD, HD)],
                send_sem=out_send.at[a],
                recv_sem=out_recv.at[a],
                device_id=(d, t),
                device_id_type=MESH,
            ).start()

        @pl.when(t == me)
        def _():
            pltpu.make_async_copy(
                tx.at[a, rows_at(t * TOK, TOK)], targets[a].at[0, :, rows_at(me * HD, HD)], out_local.at[a]
            ).start()

    def token_rows(ref, t):
        return ref[pl.ds(REST - first + t * TOK, TOK), :]

    def send_plain(a, ref):

        def body(j, carry):
            t = peer(j)
            tx[a, rows_at(t * TOK, TOK), :] = token_rows(ref, t).astype(BF16)
            send_back(a, t)
            return carry

        lax.fori_loop(0, SHARDS, body, 0)

    send_plain(0, go)

    arrived(3)
    fill(3, None)
    roll_into(gr, g_t)
    dk_t[...] = jnp.zeros_like(dk_t)
    dv_t[...] = jnp.zeros_like(dv_t)

    def backward(weights, queries_at, keys_at, out_at):
        low = weights.astype(BF16)
        grads = gr[queries_at, :]
        delta = jnp.sum(grads.astype(F32) * go[out_at, :], axis=1, keepdims=True)
        grad_probs = dot_nt(grads, vr[keys_at, :])
        grad_scores = (weights * (grad_probs - delta)).astype(BF16)
        gq[out_at, :] = dot_nn(grad_scores, kr[keys_at, :]) * SCALE
        dk_t[:, keys_at] += dot_nn(q_t[:, queries_at], grad_scores)
        dv_t[:, keys_at] += dot_nn(g_t[:, queries_at], low)

    def rest_backward(b, carry):
        backward(
            w_rest[rows_at(b * ROWS, ROWS), :],
            rows_at(BIG + b * ROWS, ROWS),
            pl.ds(BIG, REST),
            rows_at(LEN + b * ROWS, ROWS),
        )
        return carry

    lax.fori_loop(0, REST // ROWS, rest_backward, 0)

    def big_backward(b, carry):
        at = rows_at(b * ROWS, ROWS)
        backward(w_big[at, :], at, pl.ds(0, BIG), rows_at(REST + b * ROWS, ROWS))
        return carry

    lax.fori_loop(0, BIG // ROWS, big_backward, 0)

    def head(ref):
        ref[0:REST] = ref[LEN : LEN + REST]

    def turn_back(ref, turned, factor):

        def body(b, carry):
            value = turned[:, rows_at(b * ROWS, ROWS)].T
            ref[rows_at(REST + b * ROWS, ROWS), :] = value if factor is None else value * factor
            return carry

        lax.fori_loop(0, LEN // ROWS, body, 0)
        head(ref)

    def send_normed(a, source, ref, gain):

        def body(j, total):
            t = peer(j)
            unit, inverse = norm_parts(source, rows_at(t * TOK, TOK))
            grad = token_rows(ref, t)
            total = total + jnp.sum(grad * unit, axis=0, keepdims=True)
            scaled = grad * gain[...]
            inner = jnp.mean(scaled * unit, axis=1, keepdims=True)
            tx[a, rows_at(t * TOK, TOK), :] = (inverse * (scaled - unit * inner)).astype(BF16)
            send_back(a, t)
            return total

        return lax.fori_loop(0, SHARDS, body, jnp.zeros((1, HD), F32))

    gains[0] = jnp.zeros((8, HD), F32)
    head(gq)
    gains[0, 0:1, :] = send_normed(1, 0, gq, gain_q)
    turn_back(gk, dk_t, SCALE)
    gains[0, 1:2, :] = send_normed(2, 1, gk, gain_k)
    turn_back(gv, dv_t, None)
    send_plain(3, gv)

    for r in range(rounds):
        copy = pltpu.make_async_remote_copy(
            src_ref=gains.at[r],
            dst_ref=gain_rx.at[r],
            send_sem=gain_send.at[r],
            recv_sem=gain_recv.at[r],
            device_id=(partner(r), me),
            device_id_type=MESH,
        )
        copy.start()
        copy.wait()
        gains[r + 1] = gains[r] + gain_rx[r]
    ggq_out[...] = gains[rounds, 0:1, :]
    ggk_out[...] = gains[rounds, 1:2, :]

    for a in range(4):
        part = rx.at[a, pl.ds(0, LEN - TOK)]
        pltpu.make_async_copy(part, part, in_send.at[a]).wait()
        pltpu.make_async_copy(part, part, out_send.at[a]).wait()
        own = rx.at[a, pl.ds(0, TOK)]
        pltpu.make_async_copy(own, own, out_local.at[a]).wait()
        landed = targets[a].at[0, :, pl.ds(0, LEN - TOK)]
        pltpu.make_async_copy(landed, landed, out_recv.at[a]).wait()


def on_device(dp_size, query_rows, key_rows, value_rows, out_cotangent, segment_ids, gain_query, gain_key):
    rounds = dp_size.bit_length() - 1
    rows = jax.ShapeDtypeStruct((1, TOK, LEN), BF16)
    gain = jax.ShapeDtypeStruct((1, HD), F32)
    hbm = pl.BlockSpec(memory_space=pl.ANY)
    vmem = pl.BlockSpec(memory_space=pltpu.VMEM)
    smem = pl.BlockSpec(memory_space=pltpu.SMEM)
    dma = pltpu.SemaphoreType.DMA
    return pl.pallas_call(
        functools.partial(kernel, dp_size),
        out_shape=(rows, rows, rows, rows, gain, gain),
        in_specs=[hbm, hbm, hbm, hbm, smem, vmem, vmem, vmem],
        out_specs=(hbm, hbm, hbm, hbm, vmem, vmem),
        scratch_shapes=[
            pltpu.VMEM((4, LEN, HD), BF16),
            pltpu.VMEM((4, LEN, HD), BF16),
            pltpu.VMEM((LEN + REST, HD), F32),
            pltpu.VMEM((LEN, HD), BF16),
            pltpu.VMEM((LEN, HD), BF16),
            pltpu.VMEM((LEN, HD), BF16),
            pltpu.VMEM((LEN, HD), BF16),
            pltpu.VMEM((HD, LEN), BF16),
            pltpu.VMEM((HD, LEN), BF16),
            pltpu.VMEM((REST, HD), BF16),
            pltpu.VMEM((BIG, BIG), F32),
            pltpu.VMEM((REST, REST), F32),
            pltpu.VMEM((LEN + REST, HD), F32),
            pltpu.VMEM((LEN + REST, HD), F32),
            pltpu.VMEM((LEN + REST, HD), F32),
            pltpu.VMEM((LEN + REST, HD), F32),
            pltpu.VMEM((HD, LEN), F32),
            pltpu.VMEM((HD, LEN), F32),
            pltpu.VMEM((rounds + 1, 8, HD), F32),
            pltpu.VMEM((rounds + 1, 8, HD), F32),
            dma((4,)), dma((4,)), dma((4,)), dma((4,)), dma((4,)), dma((4,)),
            dma((rounds + 1,)), dma((rounds + 1,)),
        ],
        compiler_params=pltpu.CompilerParams(
            collective_id=0, has_side_effects=True, vmem_limit_bytes=56 * 2**20
        ),
    )(query_rows, key_rows, value_rows, out_cotangent, segment_ids, segment_ids, gain_query, gain_key)


def solution(mesh):
    placed = (
        P("dp", "seq", None),
        P("dp", "seq", None),
        P("dp", "seq", None),
        P("dp", "seq", None),
        P("dp", None),
        P("seq", None),
        P("seq", None),
    )
    return jax.shard_map(
        functools.partial(on_device, mesh.shape["dp"]),
        mesh=mesh,
        in_specs=placed,
        out_specs=(
            P("dp", "seq", None),
            P("dp", "seq", None),
            P("dp", "seq", None),
            P("dp", "seq", None),
            P("seq", None),
            P("seq", None),
        ),
        check_vma=False,
    )
```

profile of v0, /device:TPU:6, one launch (start us, length us, event | category | flops | bytes accessed | tf_op | source)
XLA Modules:
  0.0 71.5 jit_solution(10013436917206428697)
XLA Ops:
  0.6 64.5 %shard_map.118 = (bf16[1,128,2048]{2,1,0:T(8,128)(2,1)}, bf16[1,128,2048]{2,1,0:T(8,128)(2,1)}, bf16[1,128,2048]{2,1,0:T(8,128)(2,1)}, bf16[1,128,2048]{2,1,0:T(...) custom-call(bf16[1,128,2048]{2,1,0:T(8,128)(2,1)} %q_in.1, bf16[1,128,2048]{2,1,0:T(8,128)(2,1)} %k_in.1, ...), custom_call_target="tpu_custom_call" | custom-call | tf_op jit(solution)/shard_map/pallas_call | solution.py:332
  65.2 0.0 copy-start.2
  65.2 1.9 %copy.19 = bf16[1,128,2048]{2,1,0:T(8,128)(2,1)} copy(bf16[1,128,2048]{2,1,0:T(8,128)(2,1)} %get-tuple-element.12) | data formatting | bytes 1048576
  67.1 0.0 copy-done.2
  67.1 0.0 copy-start.1
  67.1 0.8 %copy.20 = bf16[1,128,2048]{2,1,0:T(8,128)(2,1)} copy(bf16[1,128,2048]{2,1,0:T(8,128)(2,1)S(1)} %copy-done.2) | data formatting | bytes 1048576
  67.9 0.4 copy-done.1
  68.3 0.0 copy-start
  68.3 0.8 %copy.21 = bf16[1,128,2048]{2,1,0:T(8,128)(2,1)} copy(bf16[1,128,2048]{2,1,0:T(8,128)(2,1)S(1)} %copy-done.1) | data formatting | bytes 1048576
  69.1 0.4 copy-done
  69.6 0.0 copy-start.4
  69.6 0.8 %copy.22 = bf16[1,128,2048]{2,1,0:T(8,128)(2,1)} copy(bf16[1,128,2048]{2,1,0:T(8,128)(2,1)S(1)} %copy-done) | data formatting | bytes 1048576
  70.4 0.0 copy-done.4
  70.4 0.0 copy-start.3
  70.4 0.5 copy.23
  70.9 0.2 copy-done.3
  71.0 0.5 copy.24
Async XLA Ops:
  65.2 2.0 %copy-start.2 = (bf16[1,128,2048]{2,1,0:T(8,128)(2,1)S(1)}, bf16[1,128,2048]{2,1,0:T(8,128)(2,1)}, u32[]{:S(2)}) copy-start(bf16[1,128,2048]{2,1,0:T(8,128)(2,1)} %get-tuple-element.13) | copy-start | bytes 1572868
  67.1 1.2 %copy-start.1 = (bf16[1,128,2048]{2,1,0:T(8,128)(2,1)S(1)}, bf16[1,128,2048]{2,1,0:T(8,128)(2,1)}, u32[]{:S(2)}) copy-start(bf16[1,128,2048]{2,1,0:T(8,128)(2,1)} %get-tuple-element.14) | copy-start | bytes 1572868
  68.3 1.2 %copy-start = (bf16[1,128,2048]{2,1,0:T(8,128)(2,1)S(1)}, bf16[1,128,2048]{2,1,0:T(8,128)(2,1)}, u32[]{:S(2)}) copy-start(bf16[1,128,2048]{2,1,0:T(8,128)(2,1)} %get-tuple-element.15) | copy-start | bytes 1572868
  69.6 0.8 %copy-start.4 = (f32[1,128]{1,0:T(1,128)S(1)}, f32[1,128]{1,0:T(1,128)}, u32[]{:S(2)}) copy-start(f32[1,128]{1,0:T(1,128)} %get-tuple-element.16) | copy-start | bytes 1540
  70.4 0.7 copy-start.3
where the time goes:
time: 71.8 us; the launch traced here: 71.5 us
  Pallas kernels  64.5 us (90%)
  local copies, waits for them, and re-layouts  6.37 us (9%)
    pallas_call x1, Pallas kernels, on_device(): pl.pallas_call(functools.partial(kernel, dp_size), out_shape=(rows, rows,...  64.5 us
    unnamed x16, local copies, waits for them, and re-layouts  6.37 us

commit v1 on v0

v1 whole, which is shorter than its diff:
```python
import functools
import math

import jax
import jax.numpy as jnp
from jax import lax
from jax.experimental import pallas as pl
from jax.experimental.pallas import tpu as pltpu
from jax.sharding import PartitionSpec as P

MESH = pl.DeviceIdType.MESH
EPSILON = 1e-06
NEGATIVE = -1e30
HD = 128
LEN = 2048
BIG = 1536
REST = LEN - BIG
ROWS = 256
SIDE = 4
SHARDS = SIDE * SIDE
TOK = LEN // SHARDS
GROUP = TOK * SIDE
SCALE = 1.0 / math.sqrt(HD)
EXP2_SCALE = SCALE * math.log2(math.e)
F32 = jnp.float32
BF16 = jnp.bfloat16


def dot_nt(a, b):
    return lax.dot_general(a, b, (((1,), (1,)), ((), ())), preferred_element_type=F32)


def dot_nn(a, b):
    return jnp.dot(a, b, preferred_element_type=F32)


def rows_at(start, size):
    return pl.ds(pl.multiple_of(start, size), size)


def kernel(
    dp_size,
    q_in, k_in, v_in, g_in, seg_in, gain_q_in, gain_k_in,
    o_out, dq_out, dk_out, dv_out, ggq_out, ggk_out,
    seg_s, seg_v, gain_q, gain_k, rx, tx, shifted, units, inverses, qr, kr, vr, gr, q_t, g_t, marks, p_big, p_rest, scale_of,
    go, gq, gk, gv, dk_t, dv_t, gains, gain_rx,
    in_send, in_recv, in_local, out_send, out_recv, out_local, gain_send, gain_recv, ready, small,
):
    d = lax.axis_index("dp")
    me = lax.axis_index("seq")
    mx, my = me // SIDE, me % SIDE
    rounds = dp_size.bit_length() - 1

    def peer(j):
        return (mx + j // SIDE) % SIDE * SIDE + (my + j % SIDE) % SIDE

    def upper(r):
        return (d // (1 << r)) % 2

    def partner(r):
        return d + (1 << r) - 2 * (1 << r) * upper(r)

    barrier = pltpu.get_barrier_semaphore()

    def greet(j, carry):
        pl.semaphore_signal(barrier, inc=1, device_id=(d, peer(j)), device_id_type=MESH)
        return carry

    for r in range(rounds):

        @pl.when(upper(r) == 0)
        def _(r=r):
            pl.semaphore_signal(barrier, inc=1, device_id=(partner(r), me), device_id_type=MESH)

    lax.fori_loop(1, SHARDS, greet, 0)
    pl.semaphore_wait(barrier, SHARDS - 1 + sum(upper(r) for r in range(rounds)))

    sources = (q_in, k_in, v_in, g_in)
    targets = (o_out, dq_out, dk_out, dv_out)
    for a in range(4):

        def send(j, carry, a=a):
            to = peer(j)
            pltpu.make_async_remote_copy(
                src_ref=sources[a].at[0, :, rows_at(to * HD, HD)],
                dst_ref=rx.at[a, rows_at(me * TOK, TOK)],
                send_sem=in_send.at[a],
                recv_sem=in_recv.at[a],
                device_id=(d, to),
                device_id_type=MESH,
            ).start()
            return carry

        lax.fori_loop(1, SHARDS, send, 0)
        pltpu.make_async_copy(
            sources[a].at[0, :, rows_at(me * HD, HD)], rx.at[a, rows_at(me * TOK, TOK)], in_local.at[a]
        ).start()

    for r in range(rounds):

        @pl.when(upper(r) == 1)
        def _(r=r):
            pl.semaphore_signal(ready.at[r], inc=1, device_id=(partner(r), me), device_id_type=MESH)

    fetches = [
        pltpu.make_async_copy(here, there, small.at[i])
        for i, (here, there) in enumerate(
            ((seg_in, seg_s), (seg_in, seg_v), (gain_q_in, gain_q), (gain_k_in, gain_k))
        )
    ]
    for fetch in fetches:
        fetch.start()
    for fetch in fetches:
        fetch.wait()

    image = seg_s[0, LEN // 2]

    def halve(_, held):
        low, high = held
        mid = (low + high) // 2
        inside = seg_s[0, mid] >= image
        return (jnp.where(inside, low, mid + 1), jnp.where(inside, mid, high))

    first, _ = lax.fori_loop(0, 10, halve, (jnp.int32(0), jnp.int32(REST)))

    lanes = lax.broadcasted_iota(jnp.int32, (TOK, HD), 1).astype(F32)
    for t in range(2 * REST // TOK):
        token = (BIG + t * TOK) % LEN
        numbers = seg_v[0:1, token : token + TOK].astype(F32)
        column = jnp.broadcast_to(numbers, (HD, TOK)).T
        shifted[t * TOK : (t + 1) * TOK] = jnp.where(column == lanes, 1.0, 0.0)
    marks[...] = shifted[pl.ds(first, REST), :].astype(BF16)
    dk_t[...] = jnp.zeros_like(dk_t)
    dv_t[...] = jnp.zeros_like(dv_t)
    gains[0] = jnp.zeros((8, HD), F32)

    def fill(a, gain):
        part = rx.at[a, pl.ds(0, LEN - TOK)]
        pltpu.make_async_copy(part, part, in_recv.at[a]).wait()
        own = rx.at[a, pl.ds(0, TOK)]
        pltpu.make_async_copy(own, own, in_local.at[a]).wait()
        for g in range(SIDE):
            at = pl.ds(g * GROUP, GROUP)
            x = rx[a, at, :].astype(F32)
            if gain is not None:
                inverse = lax.rsqrt(jnp.mean(x * x, axis=1, keepdims=True) + EPSILON)
                x = x * inverse
                units[a, at, :] = x
                inverses[a, at, :] = jnp.broadcast_to(inverse, (GROUP, HD))
                x = x * gain[...]
            shifted[at, :] = x
        shifted[LEN : LEN + REST] = shifted[0:REST]

    def roll_into(rolled, turned):

        def body(b, carry):
            value = shifted[pl.ds(first + b * GROUP, GROUP), :]
            rolled[rows_at(b * GROUP, GROUP), :] = value.astype(BF16)
            if turned is not None:
                turned[:, rows_at(b * GROUP, GROUP)] = value.T.astype(BF16)
            return carry

        lax.fori_loop(0, LEN // GROUP, body, 0)

    fill(0, gain_q)
    roll_into(qr, q_t)
    fill(1, gain_k)
    roll_into(kr, None)

    def powers_of(scores, at):
        top = jnp.max(scores, axis=1, keepdims=True)
        powers = jnp.exp2((scores - top) * EXP2_SCALE)
        scale_of[at, :] = jnp.broadcast_to(1.0 / jnp.sum(powers, axis=1, keepdims=True), (ROWS, HD))
        return powers

    def big_powers(b, carry):
        at = rows_at(b * ROWS, ROWS)
        p_big[at, :] = powers_of(dot_nt(qr[at, :], kr[0:BIG, :]), at)
        return carry

    lax.fori_loop(0, BIG // ROWS, big_powers, 0)

    def rest_powers(b, carry):
        at = rows_at(b * ROWS, ROWS)
        rolled_at = rows_at(BIG + b * ROWS, ROWS)
        scores = dot_nt(qr[rolled_at, :], kr[BIG:LEN, :])
        allowed = dot_nt(marks[at, :], marks[...]) > 0.5
        p_rest[at, :] = powers_of(jnp.where(allowed, scores, NEGATIVE), rolled_at)
        return carry

    lax.fori_loop(0, REST // ROWS, rest_powers, 0)

    fill(2, None)
    roll_into(vr, None)

    def big_values(b, carry):
        at = rows_at(b * ROWS, ROWS)
        low = (p_big[at, :] * scale_of[at, 0:1]).astype(BF16)
        go[rows_at(REST + b * ROWS, ROWS), :] = dot_nn(low, vr[0:BIG, :])
        return carry

    lax.fori_loop(0, BIG // ROWS, big_values, 0)

    def rest_values(b, carry):
        at = rows_at(b * ROWS, ROWS)
        low = (p_rest[at, :] * scale_of[rows_at(BIG + b * ROWS, ROWS), 0:1]).astype(BF16)
        value = dot_nn(low, vr[BIG:LEN, :])
        go[rows_at(LEN + b * ROWS, ROWS), :] = value
        go[at, :] = value
        return carry

    lax.fori_loop(0, REST // ROWS, rest_values, 0)

    def send_back(a):
        target = targets[a].at[0, :, rows_at(me * HD, HD)]

        def send(j, carry):
            to = peer(j)
            pltpu.make_async_remote_copy(
                src_ref=tx.at[a, rows_at(to * TOK, TOK)],
                dst_ref=target,
                send_sem=out_send.at[a],
                recv_sem=out_recv.at[a],
                device_id=(d, to),
                device_id_type=MESH,
            ).start()
            return carry

        lax.fori_loop(1, SHARDS, send, 0)
        pltpu.make_async_copy(tx.at[a, rows_at(me * TOK, TOK)], target, out_local.at[a]).start()

    def token_group(ref, g):
        return ref[pl.ds(REST - first + g * GROUP, GROUP), :]

    def send_plain(a, ref):
        for g in range(SIDE):
            tx[a, g * GROUP : (g + 1) * GROUP, :] = token_group(ref, g).astype(BF16)
        send_back(a)

    send_plain(0, go)

    fill(3, None)
    roll_into(gr, g_t)

    def backward(powers, queries_at, keys_at, out_at):
        weights = powers * scale_of[queries_at, 0:1]
        low = weights.astype(BF16)
        grads = gr[queries_at, :]
        delta = jnp.sum(grads.astype(F32) * go[out_at, :], axis=1, keepdims=True)
        grad_probs = dot_nt(grads, vr[keys_at, :])
        grad_scores = (weights * (grad_probs - delta)).astype(BF16)
        gq[out_at, :] = dot_nn(grad_scores, kr[keys_at, :]) * SCALE
        dk_t[:, keys_at] += dot_nn(q_t[:, queries_at], grad_scores)
        dv_t[:, keys_at] += dot_nn(g_t[:, queries_at], low)

    def rest_backward(b, carry):
        backward(
            p_rest[rows_at(b * ROWS, ROWS), :],
            rows_at(BIG + b * ROWS, ROWS),
            pl.ds(BIG, REST),
            rows_at(LEN + b * ROWS, ROWS),
        )
        return carry

    lax.fori_loop(0, REST // ROWS, rest_backward, 0)

    def big_backward(b, carry):
        at = rows_at(b * ROWS, ROWS)
        backward(p_big[at, :], at, pl.ds(0, BIG), rows_at(REST + b * ROWS, ROWS))
        return carry

    lax.fori_loop(0, BIG // ROWS, big_backward, 0)

    def head(ref):
        ref[0:REST] = ref[LEN : LEN + REST]

    def turn_back(ref, turned, factor):

        def body(b, carry):
            value = turned[:, rows_at(b * GROUP, GROUP)].T
            ref[rows_at(REST + b * GROUP, GROUP), :] = value if factor is None else value * factor
            return carry

        lax.fori_loop(0, LEN // GROUP, body, 0)
        head(ref)

    def send_normed(a, source, ref, gain):
        total = jnp.zeros((1, HD), F32)
        for g in range(SIDE):
            at = pl.ds(g * GROUP, GROUP)
            unit = units[source, at, :]
            grad = token_group(ref, g)
            total = total + jnp.sum(grad * unit, axis=0, keepdims=True)
            scaled = grad * gain[...]
            inner = jnp.mean(scaled * unit, axis=1, keepdims=True)
            tx[a, at, :] = (inverses[source, at, :] * (scaled - unit * inner)).astype(BF16)
        send_back(a)
        return total

    head(gq)
    gains[0, 0:1, :] = send_normed(1, 0, gq, gain_q)
    turn_back(gk, dk_t, SCALE)
    gains[0, 1:2, :] = send_normed(2, 1, gk, gain_k)
    turn_back(gv, dv_t, None)
    send_plain(3, gv)

    for r in range(rounds):

        @pl.when(upper(r) == 0)
        def _(r=r):
            pl.semaphore_wait(ready.at[r], 1)

        copy = pltpu.make_async_remote_copy(
            src_ref=gains.at[r],
            dst_ref=gain_rx.at[r],
            send_sem=gain_send.at[r],
            recv_sem=gain_recv.at[r],
            device_id=(partner(r), me),
            device_id_type=MESH,
        )
        copy.start()
        copy.wait()
        gains[r + 1] = gains[r] + gain_rx[r]
    ggq_out[...] = gains[rounds, 0:1, :]
    ggk_out[...] = gains[rounds, 1:2, :]

    for a in range(4):
        part = rx.at[a, pl.ds(0, LEN - TOK)]
        pltpu.make_async_copy(part, part, in_send.at[a]).wait()
        pltpu.make_async_copy(part, part, out_send.at[a]).wait()
        own = rx.at[a, pl.ds(0, TOK)]
        pltpu.make_async_copy(own, own, out_local.at[a]).wait()
        landed = targets[a].at[0, :, pl.ds(0, LEN - TOK)]
        pltpu.make_async_copy(landed, landed, out_recv.at[a]).wait()


def settle(*refs):
    held, placed, sem = refs[:6], refs[6:12], refs[12]
    copies = [pltpu.make_async_copy(held[i], placed[i], sem.at[i]) for i in range(6)]
    for copy in copies:
        copy.start()
    for copy in copies:
        copy.wait()


def on_device(dp_size, *operands):
    rounds = dp_size.bit_length() - 1
    rows = jax.ShapeDtypeStruct((1, TOK, LEN), BF16)
    gain = jax.ShapeDtypeStruct((1, HD), F32)
    hbm = pl.BlockSpec(memory_space=pltpu.HBM)
    vmem = pl.BlockSpec(memory_space=pltpu.VMEM)
    place = pl.BlockSpec(memory_space=pl.ANY)
    dma = pltpu.SemaphoreType.DMA
    spread = pltpu.VMEM((LEN + REST, HD), F32)
    packed = pltpu.VMEM((LEN, HD), BF16)
    results = pl.pallas_call(
        functools.partial(kernel, dp_size),
        out_shape=(rows, rows, rows, rows, gain, gain),
        in_specs=[hbm] * 7,
        out_specs=(place, place, place, place, vmem, vmem),
        scratch_shapes=[
            pltpu.SMEM((1, LEN), jnp.int32),
            pltpu.VMEM((1, LEN), jnp.int32),
            pltpu.VMEM((1, HD), F32),
            pltpu.VMEM((1, HD), F32),
            pltpu.VMEM((4, LEN, HD), BF16),
            pltpu.VMEM((4, LEN, HD), BF16),
            spread,
            pltpu.VMEM((2, LEN, HD), F32),
            pltpu.VMEM((2, LEN, HD), F32),
            packed, packed, packed, packed,
            pltpu.VMEM((HD, LEN), BF16),
            pltpu.VMEM((HD, LEN), BF16),
            pltpu.VMEM((REST, HD), BF16),
            pltpu.VMEM((BIG, BIG), F32),
            pltpu.VMEM((REST, REST), F32),
            pltpu.VMEM((LEN, HD), F32),
            spread, spread, spread, spread,
            pltpu.VMEM((HD, LEN), F32),
            pltpu.VMEM((HD, LEN), F32),
            pltpu.VMEM((rounds + 1, 8, HD), F32),
            pltpu.VMEM((rounds + 1, 8, HD), F32),
            dma((4,)), dma((4,)), dma((4,)), dma((4,)), dma((4,)), dma((4,)),
            dma((rounds + 1,)), dma((rounds + 1,)), pltpu.SemaphoreType.REGULAR((rounds + 1,)), dma((4,)),
        ],
        compiler_params=pltpu.CompilerParams(
            collective_id=0, has_side_effects=True, vmem_limit_bytes=48 * 2**20
        ),
    )(*(pltpu.with_memory_space_constraint(x, pltpu.HBM) for x in operands))
    return pl.pallas_call(
        settle,
        out_shape=(rows, rows, rows, rows, gain, gain),
        in_specs=[vmem] * 6,
        out_specs=(hbm,) * 6,
        scratch_shapes=[dma((6,))],
    )(*(pltpu.with_memory_space_constraint(x, pltpu.VMEM) for x in results))


def solution(mesh):
    placed = (
        P("dp", "seq", None),
        P("dp", "seq", None),
        P("dp", "seq", None),
        P("dp", "seq", None),
        P("dp", None),
        P("seq", None),
        P("seq", None),
    )
    return jax.shard_map(
        functools.partial(on_device, mesh.shape["dp"]),
        mesh=mesh,
        in_specs=placed,
        out_specs=(
            P("dp", "seq", None),
            P("dp", "seq", None),
            P("dp", "seq", None),
            P("dp", "seq", None),
            P("seq", None),
            P("seq", None),
        ),
        check_vma=False,
    )
```

time: 71.8 us -> 61.8 us (0.86)
  the two profiles are of different devices: /device:TPU:6 before, /device:TPU:192 now
where the time goes in v1:
time: 61.8 us; the launch traced here: 61.7 us
  Pallas kernels  61 us (99%)
  between operations  0.64 us (1%)
    pallas_call x1, Pallas kernels, on_device(): pl.pallas_call(functools.partial(kernel, dp_size), out_shape=(rows, rows,...  59.7 us
    pallas_call x1, Pallas kernels, on_device(): pl.pallas_call(settle, out_shape=(rows, rows, rows, rows, gain, gain), in...  1.37 us

profile of v1, /device:TPU:192, one launch (start us, length us, event | category | flops | bytes accessed | tf_op | source)
XLA Modules:
  0.0 61.7 jit_solution(5183371715378691755)
XLA Ops:
  0.6 59.7 %shard_map.118 = (bf16[1,128,2048]{2,1,0:T(8,128)(2,1)S(1)}, bf16[1,128,2048]{2,1,0:T(8,128)(2,1)S(1)}, bf16[1,128,2048]{2,1,0:T(8,128)(2,1)S(1)}, bf16[1,128,20...) custom-call(bf16[1,128,2048]{2,1,0:T(8,128)(2,1)} %q_in.1, bf16[1,128,2048]{2,1,0:T(8,128)(2,1)} %k_in.1, ...), custom_call_target="tpu_custom_call" | custom-call | tf_op jit(solution)/shard_map/pallas_call | solution.py:356
  60.3 1.4 %shard_map.119 = (bf16[1,128,2048]{2,1,0:T(8,128)(2,1)}, bf16[1,128,2048]{2,1,0:T(8,128)(2,1)}, bf16[1,128,2048]{2,1,0:T(8,128)(2,1)}, bf16[1,128,2048]{2,1,0:T(...) custom-call(bf16[1,128,2048]{2,1,0:T(8,128)(2,1)S(1)} %get-tuple-element.12.refs_0_, ...), custom_call_target="tpu_custom_call" | custom-call | tf_op jit(solution)/shard_map/pallas_call | solution.py:390

commit v2 on v1

--- a/solution.py
+++ b/solution.py
@@ -42,7 +42,7 @@
     dp_size,
     q_in, k_in, v_in, g_in, seg_in, gain_q_in, gain_k_in,
     o_out, dq_out, dk_out, dv_out, ggq_out, ggk_out,
-    seg_s, seg_v, gain_q, gain_k, rx, tx, shifted, units, inverses, qr, kr, vr, gr, q_t, g_t, marks, p_big, p_rest, scale_of,
+    seg_s, seg_v, gain_q, gain_k, rx, tx, shifted, units, inverses, qr, kr, vr, gr, q_t, g_t, marks, p_big, p_rest, low_big, low_rest, scale_of,
     go, gq, gk, gv, dk_t, dv_t, gains, gain_rx,
     in_send, in_recv, in_local, out_send, out_recv, out_local, gain_send, gain_recv, ready, small,
 ):
@@ -130,8 +130,6 @@
         column = jnp.broadcast_to(numbers, (HD, TOK)).T
         shifted[t * TOK : (t + 1) * TOK] = jnp.where(column == lanes, 1.0, 0.0)
     marks[...] = shifted[pl.ds(first, REST), :].astype(BF16)
-    dk_t[...] = jnp.zeros_like(dk_t)
-    dv_t[...] = jnp.zeros_like(dv_t)
     gains[0] = jnp.zeros((8, HD), F32)
 
     def fill(a, gain):
@@ -178,7 +176,7 @@
         p_big[at, :] = powers_of(dot_nt(qr[at, :], kr[0:BIG, :]), at)
         return carry
 
-    lax.fori_loop(0, BIG // ROWS, big_powers, 0)
+    lax.fori_loop(0, BIG // ROWS, big_powers, 0, unroll=2)
 
     def rest_powers(b, carry):
         at = rows_at(b * ROWS, ROWS)
@@ -188,7 +186,7 @@
         p_rest[at, :] = powers_of(jnp.where(allowed, scores, NEGATIVE), rolled_at)
         return carry
 
-    lax.fori_loop(0, REST // ROWS, rest_powers, 0)
+    lax.fori_loop(0, REST // ROWS, rest_powers, 0, unroll=2)
 
     fill(2, None)
     roll_into(vr, None)
@@ -196,20 +194,22 @@
     def big_values(b, carry):
         at = rows_at(b * ROWS, ROWS)
         low = (p_big[at, :] * scale_of[at, 0:1]).astype(BF16)
+        low_big[at, :] = low
         go[rows_at(REST + b * ROWS, ROWS), :] = dot_nn(low, vr[0:BIG, :])
         return carry
 
-    lax.fori_loop(0, BIG // ROWS, big_values, 0)
+    lax.fori_loop(0, BIG // ROWS, big_values, 0, unroll=2)
 
     def rest_values(b, carry):
         at = rows_at(b * ROWS, ROWS)
         low = (p_rest[at, :] * scale_of[rows_at(BIG + b * ROWS, ROWS), 0:1]).astype(BF16)
+        low_rest[at, :] = low
         value = dot_nn(low, vr[BIG:LEN, :])
         go[rows_at(LEN + b * ROWS, ROWS), :] = value
         go[at, :] = value
         return carry
 
-    lax.fori_loop(0, REST // ROWS, rest_values, 0)
+    lax.fori_loop(0, REST // ROWS, rest_values, 0, unroll=2)
 
     def send_back(a):
         target = targets[a].at[0, :, rows_at(me * HD, HD)]
@@ -242,47 +242,57 @@
     fill(3, None)
     roll_into(gr, g_t)
 
+    def head(ref):
+        ref[0:REST] = ref[LEN : LEN + REST]
+
+    def columns_of(turned, rows_t):
+
+        def body(c, carry):
+            at = rows_at(c * GROUP, GROUP)
+            turned[:, at] = dot_nn(rows_t[:, 0:BIG], low_big[:, at])
+            return carry
+
+        lax.fori_loop(0, BIG // GROUP, body, 0)
+        turned[:, BIG:LEN] = dot_nn(rows_t[:, BIG:LEN], low_rest[...])
+
+    def turn_back(ref, turned, factor):
+
+        def body(b, carry):
+            value = turned[:, rows_at(b * GROUP, GROUP)].T
+            ref[rows_at(REST + b * GROUP, GROUP), :] = value if factor is None else value * factor
+            return carry
+
+        lax.fori_loop(0, LEN // GROUP, body, 0)
+        head(ref)
+
+    columns_of(dv_t, g_t)
+    turn_back(gv, dv_t, None)
+    send_plain(3, gv)
+
     def backward(powers, queries_at, keys_at, out_at):
         weights = powers * scale_of[queries_at, 0:1]
-        low = weights.astype(BF16)
         grads = gr[queries_at, :]
         delta = jnp.sum(grads.astype(F32) * go[out_at, :], axis=1, keepdims=True)
         grad_probs = dot_nt(grads, vr[keys_at, :])
         grad_scores = (weights * (grad_probs - delta)).astype(BF16)
         gq[out_at, :] = dot_nn(grad_scores, kr[keys_at, :]) * SCALE
-        dk_t[:, keys_at] += dot_nn(q_t[:, queries_at], grad_scores)
-        dv_t[:, keys_at] += dot_nn(g_t[:, queries_at], low)
+        return grad_scores
 
     def rest_backward(b, carry):
-        backward(
-            p_rest[rows_at(b * ROWS, ROWS), :],
-            rows_at(BIG + b * ROWS, ROWS),
-            pl.ds(BIG, REST),
-            rows_at(LEN + b * ROWS, ROWS),
+        at = rows_at(b * ROWS, ROWS)
+        low_rest[at, :] = backward(
+            p_rest[at, :], rows_at(BIG + b * ROWS, ROWS), pl.ds(BIG, REST), rows_at(LEN + b * ROWS, ROWS)
         )
         return carry
 
-    lax.fori_loop(0, REST // ROWS, rest_backward, 0)
+    lax.fori_loop(0, REST // ROWS, rest_backward, 0, unroll=2)
 
     def big_backward(b, carry):
         at = rows_at(b * ROWS, ROWS)
-        backward(p_big[at, :], at, pl.ds(0, BIG), rows_at(REST + b * ROWS, ROWS))
-        return carry
-
-    lax.fori_loop(0, BIG // ROWS, big_backward, 0)
-
-    def head(ref):
-        ref[0:REST] = ref[LEN : LEN + REST]
-
-    def turn_back(ref, turned, factor):
-
-        def body(b, carry):
-            value = turned[:, rows_at(b * GROUP, GROUP)].T
-            ref[rows_at(REST + b * GROUP, GROUP), :] = value if factor is None else value * factor
-            return carry
-
-        lax.fori_loop(0, LEN // GROUP, body, 0)
-        head(ref)
+        low_big[at, :] = backward(p_big[at, :], at, pl.ds(0, BIG), rows_at(REST + b * ROWS, ROWS))
+        return carry
+
+    lax.fori_loop(0, BIG // ROWS, big_backward, 0, unroll=2)
 
     def send_normed(a, source, ref, gain):
         total = jnp.zeros((1, HD), F32)
@@ -299,10 +309,9 @@
 
     head(gq)
     gains[0, 0:1, :] = send_normed(1, 0, gq, gain_q)
+    columns_of(dk_t, q_t)
     turn_back(gk, dk_t, SCALE)
     gains[0, 1:2, :] = send_normed(2, 1, gk, gain_k)
-    turn_back(gv, dv_t, None)
-    send_plain(3, gv)
 
     for r in range(rounds):
 
@@ -374,6 +383,8 @@
             pltpu.VMEM((REST, HD), BF16),
             pltpu.VMEM((BIG, BIG), F32),
             pltpu.VMEM((REST, REST), F32),
+            pltpu.VMEM((BIG, BIG), BF16),
+            pltpu.VMEM((REST, REST), BF16),
             pltpu.VMEM((LEN, HD), F32),
             spread, spread, spread, spread,
             pltpu.VMEM((HD, LEN), F32),

time: 61.8 us -> 59.8 us (0.968)
  the two profiles are of different devices: /device:TPU:192 before, /device:TPU:6 now
where the time goes in v2:
time: 59.8 us; the launch traced here: 59.7 us
  Pallas kernels  59 us (99%)
  between operations  0.64 us (1%)
    pallas_call x1, Pallas kernels, on_device(): pl.pallas_call(functools.partial(kernel, dp_size), out_shape=(rows, rows,...  57.7 us
    pallas_call x1, Pallas kernels, on_device(): pl.pallas_call(settle, out_shape=(rows, rows, rows, rows, gain, gain), in...  1.37 us

profile of v2, /device:TPU:6, one launch (start us, length us, event | category | flops | bytes accessed | tf_op | source)
XLA Modules:
  0.0 59.7 jit_solution(9831657430845070089)
XLA Ops:
  0.6 57.7 %shard_map.118 = (bf16[1,128,2048]{2,1,0:T(8,128)(2,1)S(1)}, bf16[1,128,2048]{2,1,0:T(8,128)(2,1)S(1)}, bf16[1,128,2048]{2,1,0:T(8,128)(2,1)S(1)}, bf16[1,128,20...) custom-call(bf16[1,128,2048]{2,1,0:T(8,128)(2,1)} %q_in.1, bf16[1,128,2048]{2,1,0:T(8,128)(2,1)} %k_in.1, ...), custom_call_target="tpu_custom_call" | custom-call | tf_op jit(solution)/shard_map/pallas_call | solution.py:365
  58.3 1.4 %shard_map.119 = (bf16[1,128,2048]{2,1,0:T(8,128)(2,1)}, bf16[1,128,2048]{2,1,0:T(8,128)(2,1)}, bf16[1,128,2048]{2,1,0:T(8,128)(2,1)}, bf16[1,128,2048]{2,1,0:T(...) custom-call(bf16[1,128,2048]{2,1,0:T(8,128)(2,1)S(1)} %get-tuple-element.12.refs_0_, ...), custom_call_target="tpu_custom_call" | custom-call | tf_op jit(solution)/shard_map/pallas_call | solution.py:401

commit v3 on v2

--- a/solution.py
+++ b/solution.py
@@ -158,7 +158,7 @@
                 turned[:, rows_at(b * GROUP, GROUP)] = value.T.astype(BF16)
             return carry
 
-        lax.fori_loop(0, LEN // GROUP, body, 0)
+        lax.fori_loop(0, LEN // GROUP, body, 0, unroll=True)
 
     fill(0, gain_q)
     roll_into(qr, q_t)
@@ -252,7 +252,7 @@
             turned[:, at] = dot_nn(rows_t[:, 0:BIG], low_big[:, at])
             return carry
 
-        lax.fori_loop(0, BIG // GROUP, body, 0)
+        lax.fori_loop(0, BIG // GROUP, body, 0, unroll=True)
         turned[:, BIG:LEN] = dot_nn(rows_t[:, BIG:LEN], low_rest[...])
 
     def turn_back(ref, turned, factor):
@@ -262,7 +262,7 @@
             ref[rows_at(REST + b * GROUP, GROUP), :] = value if factor is None else value * factor
             return carry
 
-        lax.fori_loop(0, LEN // GROUP, body, 0)
+        lax.fori_loop(0, LEN // GROUP, body, 0, unroll=True)
         head(ref)
 
     columns_of(dv_t, g_t)

time: 59.8 us -> 57.6 us (0.963)
  Pallas kernels: 59 us -> 56.8 us
    pallas_call x1, Pallas kernels: 57.7 us -> 55.4 us  [on_device(): pl.pallas_call(functools.partial(kernel, dp_size), out_shape=(rows, rows,...]
where the time goes in v3:
time: 57.6 us; the launch traced here: 57.4 us
  Pallas kernels  56.8 us (99%)
  between operations  0.64 us (1%)
    pallas_call x1, Pallas kernels, on_device(): pl.pallas_call(functools.partial(kernel, dp_size), out_shape=(rows, rows,...  55.4 us
    pallas_call x1, Pallas kernels, on_device(): pl.pallas_call(settle, out_shape=(rows, rows, rows, rows, gain, gain), in...  1.37 us

profile of v3, /device:TPU:6, one launch (start us, length us, event | category | flops | bytes accessed | tf_op | source)
XLA Modules:
  0.0 57.4 jit_solution(12287533736577798953)
XLA Ops:
  0.6 55.4 %shard_map.118 = (bf16[1,128,2048]{2,1,0:T(8,128)(2,1)S(1)}, bf16[1,128,2048]{2,1,0:T(8,128)(2,1)S(1)}, bf16[1,128,2048]{2,1,0:T(8,128)(2,1)S(1)}, bf16[1,128,20...) custom-call(bf16[1,128,2048]{2,1,0:T(8,128)(2,1)} %q_in.1, bf16[1,128,2048]{2,1,0:T(8,128)(2,1)} %k_in.1, ...), custom_call_target="tpu_custom_call" | custom-call | tf_op jit(solution)/shard_map/pallas_call | solution.py:365
  56.0 1.4 %shard_map.119 = (bf16[1,128,2048]{2,1,0:T(8,128)(2,1)}, bf16[1,128,2048]{2,1,0:T(8,128)(2,1)}, bf16[1,128,2048]{2,1,0:T(8,128)(2,1)}, bf16[1,128,2048]{2,1,0:T(...) custom-call(bf16[1,128,2048]{2,1,0:T(8,128)(2,1)S(1)} %get-tuple-element.12.refs_0_, ...), custom_call_target="tpu_custom_call" | custom-call | tf_op jit(solution)/shard_map/pallas_call | solution.py:401

commit v4 on v3

--- a/solution.py
+++ b/solution.py
@@ -198,7 +198,7 @@
         go[rows_at(REST + b * ROWS, ROWS), :] = dot_nn(low, vr[0:BIG, :])
         return carry
 
-    lax.fori_loop(0, BIG // ROWS, big_values, 0, unroll=2)
+    lax.fori_loop(0, BIG // ROWS, big_values, 0, unroll=True)
 
     def rest_values(b, carry):
         at = rows_at(b * ROWS, ROWS)
@@ -209,7 +209,7 @@
         go[at, :] = value
         return carry
 
-    lax.fori_loop(0, REST // ROWS, rest_values, 0, unroll=2)
+    lax.fori_loop(0, REST // ROWS, rest_values, 0, unroll=True)
 
     def send_back(a):
         target = targets[a].at[0, :, rows_at(me * HD, HD)]
@@ -285,14 +285,14 @@
         )
         return carry
 
-    lax.fori_loop(0, REST // ROWS, rest_backward, 0, unroll=2)
+    lax.fori_loop(0, REST // ROWS, rest_backward, 0, unroll=True)
 
     def big_backward(b, carry):
         at = rows_at(b * ROWS, ROWS)
         low_big[at, :] = backward(p_big[at, :], at, pl.ds(0, BIG), rows_at(REST + b * ROWS, ROWS))
         return carry
 
-    lax.fori_loop(0, BIG // ROWS, big_backward, 0, unroll=2)
+    lax.fori_loop(0, BIG // ROWS, big_backward, 0, unroll=True)
 
     def send_normed(a, source, ref, gain):
         total = jnp.zeros((1, HD), F32)

time: 57.6 us -> 57 us (0.990)
  Pallas kernels: 56.8 us -> 56.1 us
    pallas_call x1, Pallas kernels: 55.4 us -> 54.8 us  [on_device(): pl.pallas_call(functools.partial(kernel, dp_size), out_shape=(rows, rows,...]
where the time goes in v4:
time: 57 us; the launch traced here: 56.8 us
  Pallas kernels  56.1 us (98%)
  between operations  0.64 us (1%)
    pallas_call x1, Pallas kernels, on_device(): pl.pallas_call(functools.partial(kernel, dp_size), out_shape=(rows, rows,...  54.8 us
    pallas_call x1, Pallas kernels, on_device(): pl.pallas_call(settle, out_shape=(rows, rows, rows, rows, gain, gain), in...  1.37 us

profile of v4, /device:TPU:6, one launch (start us, length us, event | category | flops | bytes accessed | tf_op | source)
XLA Modules:
  0.0 56.8 jit_solution(16753366737268832044)
XLA Ops:
  0.6 54.8 %shard_map.118 = (bf16[1,128,2048]{2,1,0:T(8,128)(2,1)S(1)}, bf16[1,128,2048]{2,1,0:T(8,128)(2,1)S(1)}, bf16[1,128,2048]{2,1,0:T(8,128)(2,1)S(1)}, bf16[1,128,20...) custom-call(bf16[1,128,2048]{2,1,0:T(8,128)(2,1)} %q_in.1, bf16[1,128,2048]{2,1,0:T(8,128)(2,1)} %k_in.1, ...), custom_call_target="tpu_custom_call" | custom-call | tf_op jit(solution)/shard_map/pallas_call | solution.py:365
  55.4 1.4 %shard_map.119 = (bf16[1,128,2048]{2,1,0:T(8,128)(2,1)}, bf16[1,128,2048]{2,1,0:T(8,128)(2,1)}, bf16[1,128,2048]{2,1,0:T(8,128)(2,1)}, bf16[1,128,2048]{2,1,0:T(...) custom-call(bf16[1,128,2048]{2,1,0:T(8,128)(2,1)S(1)} %get-tuple-element.12.refs_0_, ...), custom_call_target="tpu_custom_call" | custom-call | tf_op jit(solution)/shard_map/pallas_call | solution.py:401

commit v5 on v4

--- a/solution.py
+++ b/solution.py
@@ -66,13 +66,14 @@
         pl.semaphore_signal(barrier, inc=1, device_id=(d, peer(j)), device_id_type=MESH)
         return carry
 
+    lax.fori_loop(1, SHARDS, greet, 0, unroll=True)
+
     for r in range(rounds):
 
         @pl.when(upper(r) == 0)
         def _(r=r):
             pl.semaphore_signal(barrier, inc=1, device_id=(partner(r), me), device_id_type=MESH)
 
-    lax.fori_loop(1, SHARDS, greet, 0)
     pl.semaphore_wait(barrier, SHARDS - 1 + sum(upper(r) for r in range(rounds)))
 
     sources = (q_in, k_in, v_in, g_in)

time: 57 us -> 56.9 us (level)
  no operation moved by 1% of the time
where the time goes in v5:
time: 56.9 us; the launch traced here: 56.6 us
  Pallas kernels  56 us (98%)
  between operations  0.64 us (1%)
    pallas_call x1, Pallas kernels, on_device(): pl.pallas_call(functools.partial(kernel, dp_size), out_shape=(rows, rows,...  54.6 us
    pallas_call x1, Pallas kernels, on_device(): pl.pallas_call(settle, out_shape=(rows, rows, rows, rows, gain, gain), in...  1.37 us

profile of v5, /device:TPU:6, one launch (start us, length us, event | category | flops | bytes accessed | tf_op | source)
XLA Modules:
  0.0 56.6 jit_solution(3219175833846390204)
XLA Ops:
  0.6 54.6 %shard_map.118 = (bf16[1,128,2048]{2,1,0:T(8,128)(2,1)S(1)}, bf16[1,128,2048]{2,1,0:T(8,128)(2,1)S(1)}, bf16[1,128,2048]{2,1,0:T(8,128)(2,1)S(1)}, bf16[1,128,20...) custom-call(bf16[1,128,2048]{2,1,0:T(8,128)(2,1)} %q_in.1, bf16[1,128,2048]{2,1,0:T(8,128)(2,1)} %k_in.1, ...), custom_call_target="tpu_custom_call" | custom-call | tf_op jit(solution)/shard_map/pallas_call | solution.py:366
  55.2 1.4 %shard_map.119 = (bf16[1,128,2048]{2,1,0:T(8,128)(2,1)}, bf16[1,128,2048]{2,1,0:T(8,128)(2,1)}, bf16[1,128,2048]{2,1,0:T(8,128)(2,1)}, bf16[1,128,2048]{2,1,0:T(...) custom-call(bf16[1,128,2048]{2,1,0:T(8,128)(2,1)S(1)} %get-tuple-element.12.refs_0_, ...), custom_call_target="tpu_custom_call" | custom-call | tf_op jit(solution)/shard_map/pallas_call | solution.py:402
